TPU v7x, 32 devices: a whole 2x2x4 slice. The times are simulated.
32 devices in a mesh: region: 2 (over y), visit: 8 (over z, x), tile: 2 (over core).
Axes of the slice: x: 2, y: 2, z: 4, core: 2. Of those that a mesh axis runs over, the one named last changes fastest.
Arguments:
- science: bfloat16 [16, 8, 32, 512], P(('region', 'visit'), None, None, 'tile'), parts along dimension 0, may hold values from -6 to 6
- warped: bfloat16 [16, 8, 32, 512], P(('region', 'visit'), None, None, 'tile'), parts along dimension 0, may hold values from -6 to 6
- weights: float32 [16], P('region'), parts along dimension 0, may hold values from 0.2 to 5
- coef: float32 [16, 8, 13, 6], P(('region', 'visit')), parts along dimension 0, may hold values from -3 to 3
- basis_rows: bfloat16 [13, 17], replicated, may hold values from -1.5 to 1.5
- basis_cols: bfloat16 [13, 17], replicated, may hold values from -1.5 to 1.5
- covered: int32 [16, 8], P('region'), parts along dimension 0, may hold values from 0 to 7, all different within a row
- owner: int32 [16], P('region'), parts along dimension 0, may hold values from 0 to 7, each once
Outputs:
- templates: bfloat16 [16, 32, 512], P(('region', 'visit'), None, 'tile'), parts along dimension 0
- difference: float32 [16, 8, 32, 512], P(('region', 'visit'), None, None, 'tile'), parts along dimension 0
There are 2 independent parts, one for each index of `region`. A program takes and returns all parts, laid end to end along the dimension named above; an argument that names none is the same for every part. Nothing has to cross between parts.
Inputs may be any that keep to these rules, and one draw needn't show every extreme that they name: `covered`: each row names 8 different tiles, and every tile is named by some row. `owner`: each slot once.
All inputs are finite; a program needn't handle non-finite values.
Results may differ from a plain program's by a relative error of at most 0.0022.
Values may be sent and summed in bfloat16 or wider, within the bound.
A program may use at most 64 MiB of HBM per device.

v0:
```python
import jax
import jax.numpy as jnp
from jax import lax
from jax.sharding import PartitionSpec as P


def padded(block, sides, width):
    for axis, dim in sides:
        count = lax.axis_size(axis)
        forward = [(i, i + 1) for i in range(count - 1)]
        backward = [(target, source) for source, target in forward]
        low = lax.ppermute(
            lax.slice_in_dim(block, block.shape[dim] - width, None, axis=dim), axis, forward
        )
        high = lax.ppermute(lax.slice_in_dim(block, 0, width, axis=dim), axis, backward)
        block = jnp.concatenate([low, block, high], axis=dim)
    return block


def polynomials(rows, half, offset, total):
    yn = (2.0 * jnp.arange(rows, dtype=jnp.float32) + 1.0) / rows - 1.0
    columns = (offset + lax.iota(jnp.int32, half)).astype(jnp.float32)
    xn = (2.0 * columns + 1.0) / total - 1.0
    ygrid = jnp.broadcast_to(yn[:, None], (rows, half))
    xgrid = jnp.broadcast_to(xn[None, :], (rows, half))
    ones = jnp.ones((rows, half), jnp.float32)
    return jnp.stack([ones, xgrid, ygrid, xgrid * xgrid, xgrid * ygrid, ygrid * ygrid])


def band_matrix(profile, offsets):
    band = jnp.zeros((profile.shape[0],) + offsets.shape, jnp.bfloat16)
    for i in range(profile.shape[1]):
        band = jnp.where((offsets == i)[None], profile[:, i][:, None, None], band)
    return band


def body(science, warped, weights, coef, basis_rows, basis_cols, covered, owner):
    count, rows, half = (warped.shape[1], warped.shape[2], warped.shape[3])
    tiles = owner.shape[0]
    visit_count = lax.axis_size("visit")
    visit_here = lax.axis_index("visit")
    side_here = lax.axis_index("tile")
    side_count = lax.axis_size("tile")
    tile_dev = tiles // visit_count
    ksize = basis_rows.shape[1]
    reach = ksize // 2
    width = half + 2 * reach
    mine_over = lax.dynamic_slice_in_dim(covered, visit_here, 1, 0)[0]
    slot_of = jnp.take(owner, mine_over)
    flat_pixels = warped[0].reshape(count, rows * half)
    weight_sum = jax.ops.segment_sum(
        jnp.repeat(weights, covered.shape[1]), covered.reshape(-1), tiles
    )
    slot_weight = jax.ops.segment_sum(weight_sum, owner, tiles)
    wanted = lax.iota(jnp.int32, tiles)
    select = (slot_of[None, :] == wanted[:, None]).astype(jnp.bfloat16)
    packed = jnp.dot(select, flat_pixels, preferred_element_type=jnp.float32).astype(jnp.bfloat16)
    received = lax.all_to_all(packed, "visit", split_axis=0, concat_axis=0, tiled=True)
    received = received.reshape(visit_count, tile_dev, rows * half)
    total = jnp.sum(weights[:, None, None] * received.astype(jnp.float32), axis=0)
    mine_weight = lax.dynamic_slice_in_dim(slot_weight, visit_here * tile_dev, tile_dev, 0)
    templates = (total / mine_weight[:, None]).astype(jnp.bfloat16).reshape(tile_dev, rows, half)
    library = lax.all_gather(templates, "visit", axis=0, tiled=True)
    chosen = jnp.take(library, slot_of, axis=0)
    chosen = padded(chosen, (("tile", 2),), reach)
    row_offsets = lax.iota(jnp.int32, rows)[None, :] - lax.iota(jnp.int32, rows)[:, None] + reach
    row_band = band_matrix(basis_rows, row_offsets)
    col_offsets = lax.iota(jnp.int32, width)[:, None] - lax.iota(jnp.int32, half)[None, :]
    col_band = band_matrix(basis_cols, col_offsets)
    polys = polynomials(rows, half, side_here * half, half * side_count)
    pairs = count // 2
    tpl_blocks = chosen.reshape(pairs, 2, rows, width)
    sci_blocks = science[0].reshape(pairs, 2, rows, half)
    coef_blocks = coef[0].reshape(pairs, 2, coef.shape[2], coef.shape[3])

    def match(item):
        tpl, sci, cf = item
        blurred = jnp.einsum(
            "byz,kzx->kbyx", row_band, tpl, preferred_element_type=jnp.float32
        ).astype(jnp.bfloat16)
        smooth = jnp.einsum("kbyx,bxw->kbyw", blurred, col_band, preferred_element_type=jnp.float32)
        factor = jnp.einsum("kbp,pyw->kbyw", cf, polys, precision=lax.Precision.HIGHEST)
        return sci.astype(jnp.float32) - jnp.sum(factor * smooth, axis=1)

    difference = lax.map(match, (tpl_blocks, sci_blocks, coef_blocks)).reshape(1, count, rows, half)
    return (templates, difference)


def solution(mesh):
    in_specs = (
        P(("region", "visit"), None, None, "tile"),
        P(("region", "visit"), None, None, "tile"),
        P("region"),
        P(("region", "visit"), None, None, None),
        P(),
        P(),
        P("region", None),
        P("region"),
    )
    out_specs = (P(("region", "visit"), None, "tile"), P(("region", "visit"), None, None, "tile"))
    return jax.shard_map(body, mesh=mesh, in_specs=in_specs, out_specs=out_specs, check_vma=False)
```

profile of v0, /device:TPU:1, one launch (start us, length us, event | category | flops | bytes accessed | tf_op | source)
XLA Modules:
  0.0 80.9 jit_solution(13842811680219769208)
XLA Ops:
  0.6 0.7 fusion.223
  1.3 1.0 %copy.20 = bf16[1,8,32,256]{3,1,2,0:T(8,128)(2,1)S(1)} copy(bf16[1,8,32,256]{3,2,1,0:T(8,128)(2,1)} %param.11) | data formatting | bytes 262144
  2.3 1.3 %gather_fusion = s32[8]{0:T(128)S(1)} fusion(s32[8]{0:T(128)} %param.17, s32[1024]{0:T(1024)S(1)} %pad_clamp_fusion.1), kind=kCustom, calls=%fused_computation | custom fusion | bytes 96 | tf_op jit(solution)/shard_map/jit(_take)/gather | solution.py:49
  3.6 0.2 fusion.179
  3.8 0.5 broadcast.669
  4.3 0.7 reduce.69
  5.0 0.7 reshape.649
  5.8 6.5 %all-to-all-start = ((bf16[8,2,4096]{2,1,0:T(2,128)(2,1)}), bf16[8,2,4096]{2,1,0:T(2,128)(2,1)S(1)}, u32[]{:S(2)}, u32[]{:S(2)}) async-start(bf16[8,2,4096]{2,1,0:T(2,128)(2,1)} %reshape.649), calls=%async_computation | async-start | bytes 262144 | tf_op jit(solution)/shard_map/all_to_all | solution.py:58
  12.3 0.1 fusion.194
  12.6 0.1 fusion.188
  12.6 0.1 fusion.190
  13.0 0.3 slice_reduce_fusion.16
  13.3 0.3 slice_reduce_fusion.33
  13.7 0.1 reshape.590
  13.8 0.1 broadcast_in_dim.500
  13.8 0.1 reshape.592
  13.9 1.0 %scatter_custom_fusion = f32[8]{0:T(128)S(1)} fusion(s32[64]{0:T(128)S(1)} %reshape.590, f32[64]{0:T(128)S(1)} %reshape.592, f32[]{:T(128)} %constant.43.clone.1), kind=kCustom, calls=%fused_computation.223 | custom fusion | flops 64 | bytes 36 | tf_op jit(solution)/shard_map/scatter-add | solution.py:51
  14.9 0.7 scatter_custom_fusion.1
  15.6 0.6 dynamic_slice.19
  16.2 0.1 broadcast_multiply_fusion
  16.4 2.1 %all-to-all-done = bf16[8,2,4096]{2,1,0:T(2,128)(2,1)S(1)} async-done(((bf16[8,2,4096]{2,1,0:T(2,128)(2,1)}), bf16[8,2,4096]{2,1,0:T(2,128)(2,1)S(1)}, u32[]{:S(2)}, u32[]{:S(2)}) %all-to-all-start) | async-done | bytes 131104 | tf_op jit(solution)/shard_map/all_to_all | solution.py:58
  18.4 0.1 reshape.650
  18.6 0.4 multiply_reduce_fusion
  19.0 0.7 divide_convert_fusion
  19.7 24.5 %all_gather.3 = bf16[8,32,256]{2,1,0:T(8,128)(2,1)S(1)} all-gather(bf16[1,32,256]{2,1,0:T(8,128)(2,1)S(1)} %convert_element_type.44), channel_id=1, replica_groups=mesh['region'=2,'visit'=8,'tile'=2] {'visit'}, dimensions={0}, use_global_device_ids=true | all-gather | bytes 147456 | tf_op jit(solution)/shard_map/all_gather | solution.py:63
  44.2 0.6 gather_fusion.1
  44.8 0.1 broadcast_select_fusion
  44.9 0.1 fusion.224
  44.9 1.3 %collective-permute-start = (bf16[8,32,8]{2,1,0:T(8,128)(2,1)S(1)}, bf16[8,32,8]{2,1,0:T(8,128)(2,1)S(1)}, u32[]{:S(2)}, u32[]{:S(2)}) collective-permute-start(bf16[8,32,8]{2,1,0:T(8,128)(2,1)S(1)} %get-tuple-element.448), channel_id=1, source_target_pairs={{0,1},{2,3},{4,5},{6,7},{8,9},{10,11},{12,13},{14,15},{16,17},{18,... | collective-permute-start | bytes 12296 | tf_op jit(solution)/shard_map/ppermute | solution.py:12
  46.2 10.1 %collective-permute-start.1 = (bf16[8,32,8]{2,1,0:T(8,128)(2,1)S(1)}, bf16[8,32,8]{2,1,0:T(8,128)(2,1)S(1)}, u32[]{:S(2)}, u32[]{:S(2)}) collective-permute-start(bf16[8,32,8]{2,1,0:T(8,128)(2,1)S(1)} %get-tuple-element.449), channel_id=1, source_target_pairs={{1,0},{3,2},{5,4},{7,6},{9,8},{11,10},{13,12},{15,14},{17,16},{19,... | collective-permute-start | bytes 12296 | tf_op jit(solution)/shard_map/ppermute | solution.py:15
  56.5 0.1 stack_broadcast_in_dim.17
  56.6 0.1 stack.11
  56.7 0.3 stack.12
  57.0 0.2 collective-permute-done.1
  57.3 0.1 pad_maximum_fusion
  57.4 23.4 %while.11 = (s32[]{:T(128)}, f32[4,2,32,256]{3,2,1,0:T(8,128)}, bf16[4,2,32,256]{3,2,1,0:T(8,128)(2,1)}, f32[4,2,13,6]{2,3,1,0:T(8,128)S(1)}, f32[6,32,256]{2,0,...) while((s32[]{:T(128)}, f32[4,2,32,256]{3,2,1,0:T(8,128)}, ...), condition=%wide.region_5.6_spmd.clone, body=%wide.region_3.5_spmd.clone.sunk | while | flops 161970176 | bytes 3524725 | solution.py:85
  57.5 2.9 %fusion.239 = f32[13,2,32,256]{3,2,1,0:T(8,128)S(1)} fusion(pred[272,256]{1,0:T(8,128)(4,1)S(1)} %get-tuple-element.1120, pred[272,256]{1,0:T(8,128)(4,1)S(1)} %get-tuple-element.1122, pred[272,256]{1,0:T(8,128)(4,1)S(1)} %get-tuple-element.1124, pred[272,256]{1,0:T(8,128)(4,1)S(1)} %get-tuple-element.1126, ...), kind=kOutput, calls=%fused_computation.6.clone.1 | convolution fusion | flops 146192384 | bytes 2171908 | tf_op jit(solution)/shard_map/while/body/eval_jaxpr/kbyx,bxw->kbyw/dot_general | solution.py:81
  60.4 1.6 %fusion.240 = f32[2,32,256]{2,1,0:T(8,128)S(1)} fusion(f32[13,2,32,256]{3,2,1,0:T(8,128)S(1)} %fusion.239, f32[6,32,256]{2,0,1:T(8,128)S(1)} %get-tuple-element.1083, f32[4,2,13,6]{2,3,1,0:T(8,128)S(1)} %get-tuple-element.1082, s32[]{:T(128)} %get-tuple-element.1004), kind=kOutput, calls=%fused_computation.45.clone.1 | convolution fusion | flops 15745024 | bytes 1187844 | tf_op jit(solution)/shard_map/while/body/eval_jaxpr/kbp,pyw->kbyw/dot_general | solution.py:82
  61.9 1.4 %fusion.241 = f32[4,2,32,256]{3,2,1,0:T(8,128)} fusion(f32[4,2,32,256]{3,2,1,0:T(8,128)} %get-tuple-element.1005, s32[]{:T(128)} %get-tuple-element.1004, f32[2,32,256]{2,1,0:T(8,128)S(1)} %fusion.240, bf16[4,2,32,256]{3,2,1,0:T(8,128)(2,1)} %get-tuple-element.1081), kind=kLoop, calls=%fused_computation.101.clone.1 | loop fusion | flops 32768 | bytes 164352 | tf_op jit(solution)/shard_map/while/body/jit(dynamic_update_index_in_dim)/dynamic_update_slice | solution.py:85
  63.3 2.9 %fusion.239 = f32[13,2,32,256]{3,2,1,0:T(8,128)S(1)} fusion(pred[272,256]{1,0:T(8,128)(4,1)S(1)} %get-tuple-element.1120, pred[272,256]{1,0:T(8,128)(4,1)S(1)} %get-tuple-element.1122, pred[272,256]{1,0:T(8,128)(4,1)S(1)} %get-tuple-element.1124, pred[272,256]{1,0:T(8,128)(4,1)S(1)} %get-tuple-element.1126, ...), kind=kOutput, calls=%fused_computation.6.clone.1 | convolution fusion | flops 146192384 | bytes 2171908 | tf_op jit(solution)/shard_map/while/body/eval_jaxpr/kbyx,bxw->kbyw/dot_general | solution.py:81
  66.2 1.6 %fusion.240 = f32[2,32,256]{2,1,0:T(8,128)S(1)} fusion(f32[13,2,32,256]{3,2,1,0:T(8,128)S(1)} %fusion.239, f32[6,32,256]{2,0,1:T(8,128)S(1)} %get-tuple-element.1083, f32[4,2,13,6]{2,3,1,0:T(8,128)S(1)} %get-tuple-element.1082, s32[]{:T(128)} %get-tuple-element.1004), kind=kOutput, calls=%fused_computation.45.clone.1 | convolution fusion | flops 15745024 | bytes 1187844 | tf_op jit(solution)/shard_map/while/body/eval_jaxpr/kbp,pyw->kbyw/dot_general | solution.py:82
  67.8 1.4 %fusion.241 = f32[4,2,32,256]{3,2,1,0:T(8,128)} fusion(f32[4,2,32,256]{3,2,1,0:T(8,128)} %get-tuple-element.1005, s32[]{:T(128)} %get-tuple-element.1004, f32[2,32,256]{2,1,0:T(8,128)S(1)} %fusion.240, bf16[4,2,32,256]{3,2,1,0:T(8,128)(2,1)} %get-tuple-element.1081), kind=kLoop, calls=%fused_computation.101.clone.1 | loop fusion | flops 32768 | bytes 164352 | tf_op jit(solution)/shard_map/while/body/jit(dynamic_update_index_in_dim)/dynamic_update_slice | solution.py:85
  69.2 2.9 %fusion.239 = f32[13,2,32,256]{3,2,1,0:T(8,128)S(1)} fusion(pred[272,256]{1,0:T(8,128)(4,1)S(1)} %get-tuple-element.1120, pred[272,256]{1,0:T(8,128)(4,1)S(1)} %get-tuple-element.1122, pred[272,256]{1,0:T(8,128)(4,1)S(1)} %get-tuple-element.1124, pred[272,256]{1,0:T(8,128)(4,1)S(1)} %get-tuple-element.1126, ...), kind=kOutput, calls=%fused_computation.6.clone.1 | convolution fusion | flops 146192384 | bytes 2171908 | tf_op jit(solution)/shard_map/while/body/eval_jaxpr/kbyx,bxw->kbyw/dot_general | solution.py:81
  72.1 1.6 %fusion.240 = f32[2,32,256]{2,1,0:T(8,128)S(1)} fusion(f32[13,2,32,256]{3,2,1,0:T(8,128)S(1)} %fusion.239, f32[6,32,256]{2,0,1:T(8,128)S(1)} %get-tuple-element.1083, f32[4,2,13,6]{2,3,1,0:T(8,128)S(1)} %get-tuple-element.1082, s32[]{:T(128)} %get-tuple-element.1004), kind=kOutput, calls=%fused_computation.45.clone.1 | convolution fusion | flops 15745024 | bytes 1187844 | tf_op jit(solution)/shard_map/while/body/eval_jaxpr/kbp,pyw->kbyw/dot_general | solution.py:82
  73.6 1.4 %fusion.241 = f32[4,2,32,256]{3,2,1,0:T(8,128)} fusion(f32[4,2,32,256]{3,2,1,0:T(8,128)} %get-tuple-element.1005, s32[]{:T(128)} %get-tuple-element.1004, f32[2,32,256]{2,1,0:T(8,128)S(1)} %fusion.240, bf16[4,2,32,256]{3,2,1,0:T(8,128)(2,1)} %get-tuple-element.1081), kind=kLoop, calls=%fused_computation.101.clone.1 | loop fusion | flops 32768 | bytes 164352 | tf_op jit(solution)/shard_map/while/body/jit(dynamic_update_index_in_dim)/dynamic_update_slice | solution.py:85
  75.0 2.9 %fusion.239 = f32[13,2,32,256]{3,2,1,0:T(8,128)S(1)} fusion(pred[272,256]{1,0:T(8,128)(4,1)S(1)} %get-tuple-element.1120, pred[272,256]{1,0:T(8,128)(4,1)S(1)} %get-tuple-element.1122, pred[272,256]{1,0:T(8,128)(4,1)S(1)} %get-tuple-element.1124, pred[272,256]{1,0:T(8,128)(4,1)S(1)} %get-tuple-element.1126, ...), kind=kOutput, calls=%fused_computation.6.clone.1 | convolution fusion | flops 146192384 | bytes 2171908 | tf_op jit(solution)/shard_map/while/body/eval_jaxpr/kbyx,bxw->kbyw/dot_general | solution.py:81
  77.9 1.6 %fusion.240 = f32[2,32,256]{2,1,0:T(8,128)S(1)} fusion(f32[13,2,32,256]{3,2,1,0:T(8,128)S(1)} %fusion.239, f32[6,32,256]{2,0,1:T(8,128)S(1)} %get-tuple-element.1083, f32[4,2,13,6]{2,3,1,0:T(8,128)S(1)} %get-tuple-element.1082, s32[]{:T(128)} %get-tuple-element.1004), kind=kOutput, calls=%fused_computation.45.clone.1 | convolution fusion | flops 15745024 | bytes 1187844 | tf_op jit(solution)/shard_map/while/body/eval_jaxpr/kbp,pyw->kbyw/dot_general | solution.py:82
  79.5 1.4 %fusion.241 = f32[4,2,32,256]{3,2,1,0:T(8,128)} fusion(f32[4,2,32,256]{3,2,1,0:T(8,128)} %get-tuple-element.1005, s32[]{:T(128)} %get-tuple-element.1004, f32[2,32,256]{2,1,0:T(8,128)S(1)} %fusion.240, bf16[4,2,32,256]{3,2,1,0:T(8,128)(2,1)} %get-tuple-element.1081), kind=kLoop, calls=%fused_computation.101.clone.1 | loop fusion | flops 32768 | bytes 164352 | tf_op jit(solution)/shard_map/while/body/jit(dynamic_update_index_in_dim)/dynamic_update_slice | solution.py:85
  (42 shorter events, 0.6 us)
Async XLA Ops:
  5.0 8.0 %copy-start = (bf16[13,17]{1,0:T(8,128)(2,1)S(1)}, bf16[13,17]{1,0:T(8,128)(2,1)}, u32[]{:S(2)}) copy-start(bf16[13,17]{1,0:T(8,128)(2,1)} %param.15) | copy-start | bytes 1330
  5.7 7.6 %copy-start.1 = (bf16[13,17]{1,0:T(8,128)(2,1)S(1)}, bf16[13,17]{1,0:T(8,128)(2,1)}, u32[]{:S(2)}) copy-start(bf16[13,17]{1,0:T(8,128)(2,1)} %param.14) | copy-start | bytes 1330
  5.7 7.9 %copy-start.4 = (s32[8,8]{1,0:T(8,128)S(1)}, s32[8,8]{1,0:T(8,128)}, u32[]{:S(2)}) copy-start(s32[8,8]{1,0:T(8,128)} %param.16) | copy-start | bytes 772
  5.7 8.0 %copy-start.5 = (f32[8]{0:T(128)S(1)}, f32[8]{0:T(128)}, u32[]{:S(2)}) copy-start(f32[8]{0:T(128)} %param.12) | copy-start | bytes 100
  5.8 12.7 %all-to-all-start = ((bf16[8,2,4096]{2,1,0:T(2,128)(2,1)}), bf16[8,2,4096]{2,1,0:T(2,128)(2,1)S(1)}, u32[]{:S(2)}, u32[]{:S(2)}) async-start(bf16[8,2,4096]{2,1,0:T(2,128)(2,1)} %reshape.649), calls=%async_computation | async-start | bytes 262144 | tf_op jit(solution)/shard_map/all_to_all | solution.py:58
  16.3 40.1 %copy-start.3 = (f32[1,8,13,6]{2,1,3,0:T(8,128)S(1)}, f32[1,8,13,6]{2,1,3,0:T(8,128)}, u32[]{:S(2)}) copy-start(f32[1,8,13,6]{2,1,3,0:T(8,128)} %param.13) | copy-start | bytes 7492
  19.7 37.8 %copy-start.2 = (bf16[1,32,256]{2,1,0:T(8,128)(2,1)}, bf16[1,32,256]{2,1,0:T(8,128)(2,1)S(1)}, u32[]{:S(2)}) copy-start(bf16[1,32,256]{2,1,0:T(8,128)(2,1)S(1)} %convert_element_type.44) | copy-start | bytes 49156
  44.9 12.1 %collective-permute-start = (bf16[8,32,8]{2,1,0:T(8,128)(2,1)S(1)}, bf16[8,32,8]{2,1,0:T(8,128)(2,1)S(1)}, u32[]{:S(2)}, u32[]{:S(2)}) collective-permute-start(bf16[8,32,8]{2,1,0:T(8,128)(2,1)S(1)} %get-tuple-element.448), channel_id=1, source_target_pairs={{0,1},{2,3},{4,5},{6,7},{8,9},{10,11},{12,13},{14,15},{16,17},{18,... | collective-permute-start | bytes 12296 | tf_op jit(solution)/shard_map/ppermute | solution.py:12
  46.2 11.0 %collective-permute-start.1 = (bf16[8,32,8]{2,1,0:T(8,128)(2,1)S(1)}, bf16[8,32,8]{2,1,0:T(8,128)(2,1)S(1)}, u32[]{:S(2)}, u32[]{:S(2)}) collective-permute-start(bf16[8,32,8]{2,1,0:T(8,128)(2,1)S(1)} %get-tuple-element.449), channel_id=1, source_target_pairs={{1,0},{3,2},{5,4},{7,6},{9,8},{11,10},{13,12},{15,14},{17,16},{19,... | collective-permute-start | bytes 12296 | tf_op jit(solution)/shard_map/ppermute | solution.py:15
where the time goes:
time: 81.8 us; the launch traced here: 80.9 us
  blocking collectives  24.5 us (30%)
  matrix products  17.9 us (22%)
  starting transfers between devices  17.9 us (22%)
  other arithmetic  10.7 us (13%)
  local copies, waits for them, and re-layouts  6.37 us (8%)
  waiting for transfers between devices  2.33 us (3%)
  between operations  1.02 us (1%)
    all_gather x1, blocking collectives, body(): library = lax.all_gather(templates, 'visit', axis=0, tiled=True)  24.5 us
    dot_general x4, matrix products, match(): jnp.einsum('kbyx,bxw->kbyw', blurred, col_band, preferred_element_type=jn...  11.5 us
    ppermute x1, starting transfers between devices, padded(): lax.ppermute(lax.slice_in_dim(block, 0, width, axis=dim), axis, backward)  10.1 us
    all_to_all x1, starting transfers between devices, body(): lax.all_to_all(packed, 'visit', split_axis=0, concat_axis=0, tiled=True)  6.49 us
    dot_general x4, matrix products, match(): jnp.einsum('kbp,pyw->kbyw', cf, polys, precision=lax.Precision.HIGHEST)  6.3 us
    dynamic_update_slice x4, other arithmetic, body(): lax.map(match, (tpl_blocks, sci_blocks, coef_blocks))  5.61 us
    all_to_all x1, waiting for transfers between devices, body(): lax.all_to_all(packed, 'visit', split_axis=0, concat_axis=0, tiled=True)  2.1 us
    unnamed x16, local copies, waits for them, and re-layouts  1.87 us
  transfers between devices with their start and end apart: 3, of which 2 were waited for; matrix products, arithmetic and copies ran while one was open for 6% of the time, Pallas kernels for 0%

commit v1 on v0

--- a/solution.py
+++ b/solution.py
@@ -1,7 +1,14 @@
+import functools
+
 import jax
 import jax.numpy as jnp
 from jax import lax
+from jax.experimental import pallas as pl
+from jax.experimental.pallas import tpu as pltpu
 from jax.sharding import PartitionSpec as P
+
+MESH = pl.DeviceIdType.MESH
+LANES = 128
 
 
 def padded(block, sides, width):
@@ -34,7 +41,7 @@
     return band
 
 
-def body(science, warped, weights, coef, basis_rows, basis_cols, covered, owner):
+def sparse_body(science, warped, weights, coef, basis_rows, basis_cols, covered, owner):
     count, rows, half = (warped.shape[1], warped.shape[2], warped.shape[3])
     tiles = owner.shape[0]
     visit_count = lax.axis_size("visit")
@@ -45,14 +52,12 @@
     ksize = basis_rows.shape[1]
     reach = ksize // 2
     width = half + 2 * reach
-    mine_over = lax.dynamic_slice_in_dim(covered, visit_here, 1, 0)[0]
-    slot_of = jnp.take(owner, mine_over)
+    wanted = lax.iota(jnp.int32, tiles)
+    slots = jnp.take(owner, covered)
+    slot_of = lax.dynamic_slice_in_dim(slots, visit_here, 1, 0)[0]
+    hits = (slots[:, :, None] == wanted).astype(jnp.float32)
+    slot_weight = jnp.sum(weights[:, None, None] * hits, axis=(0, 1))
     flat_pixels = warped[0].reshape(count, rows * half)
-    weight_sum = jax.ops.segment_sum(
-        jnp.repeat(weights, covered.shape[1]), covered.reshape(-1), tiles
-    )
-    slot_weight = jax.ops.segment_sum(weight_sum, owner, tiles)
-    wanted = lax.iota(jnp.int32, tiles)
     select = (slot_of[None, :] == wanted[:, None]).astype(jnp.bfloat16)
     packed = jnp.dot(select, flat_pixels, preferred_element_type=jnp.float32).astype(jnp.bfloat16)
     received = lax.all_to_all(packed, "visit", split_axis=0, concat_axis=0, tiled=True)
@@ -86,6 +91,275 @@
     return (templates, difference)
 
 
+def match_kernel(
+    n,
+    warped_hbm,
+    coef_ref,
+    rows_ref,
+    cols_ref,
+    weights_ref,
+    covered_ref,
+    owner_ref,
+    templates_ref,
+    model_ref,
+    warped,
+    packed,
+    received,
+    library,
+    edges,
+    chosen,
+    profiles,
+    row_band,
+    col_band,
+    factor,
+    blurred,
+    load_sem,
+    send1,
+    recv1,
+    send2,
+    recv2,
+    send3,
+    recv3,
+):
+    count, rows, half = warped.shape
+    basis, ksize = rows_ref.shape
+    reach = ksize // 2
+    me = lax.axis_index("visit")
+    side = lax.axis_index("tile")
+    group = LANES // rows
+    groups = count // group
+
+    load = pltpu.make_async_copy(warped_hbm.at[0], warped, load_sem)
+    load.start()
+    barrier = pltpu.get_barrier_semaphore()
+    for d in range(1, n):
+        pl.semaphore_signal(
+            barrier, inc=1, device_id={"visit": lax.rem(me + d, n)}, device_id_type=MESH
+        )
+    pl.semaphore_signal(barrier, inc=1, device_id={"tile": 1 - side}, device_id_type=MESH)
+
+    slots = [owner_ref[covered_ref[me, k]] for k in range(count)]
+    load.wait()
+    for d in range(n):
+        target = lax.rem(me + d, n)
+        k_of = jnp.int32(0)
+        for k in range(1, count):
+            k_of = jnp.where(slots[k] == target, jnp.int32(k), k_of)
+        packed[d] = warped[k_of]
+    pl.semaphore_wait(barrier, n)
+
+    exchange = []
+    for d in range(1, n):
+        exchange.append(
+            pltpu.make_async_remote_copy(
+                src_ref=packed.at[d],
+                dst_ref=received.at[d],
+                send_sem=send1.at[d],
+                recv_sem=recv1.at[d],
+                device_id={"visit": lax.rem(me + d, n)},
+                device_id_type=MESH,
+            )
+        )
+        exchange[-1].start()
+
+    profiles[...] = jnp.zeros_like(profiles)
+    profiles[0, 0:basis, 0:ksize] = rows_ref[...].astype(jnp.float32)
+    profiles[1, 0:basis, 0:ksize] = cols_ref[...].astype(jnp.float32)
+    zi = lax.broadcasted_iota(jnp.int32, (LANES, LANES), 0)
+    xi = lax.broadcasted_iota(jnp.int32, (LANES, LANES), 1)
+    flip = (zi + xi == ksize - 1).astype(jnp.bfloat16)
+    profiles[1] = jnp.dot(
+        profiles[1].astype(jnp.bfloat16), flip, preferred_element_type=jnp.float32
+    )
+    same = (zi // rows) == (xi // rows)
+    centre = jnp.abs(zi - xi) <= reach
+    above = zi - xi > LANES // 2
+    below = xi - zi > LANES // 2
+    zero = jnp.zeros((LANES, LANES), jnp.float32)
+
+    def circulant(which, b):
+        line = jnp.broadcast_to(profiles[which, b : b + 1, :], (LANES, LANES))
+        return pltpu.roll(line, LANES - reach, 1, stride=1, stride_axis=0)
+
+    for b in range(basis):
+        row_band[b * LANES : (b + 1) * LANES, :] = jnp.where(same, circulant(0, b), zero).astype(
+            jnp.bfloat16
+        )
+        ring = circulant(1, b)
+        diagonal = jnp.where(centre, ring, zero).astype(jnp.bfloat16)
+        upper = jnp.where(above, ring, zero)
+        lower = jnp.where(below, ring, zero)
+        for j in range(half // LANES):
+            for i in range(half // LANES):
+                block = (
+                    diagonal
+                    if i == j
+                    else upper.astype(jnp.bfloat16)
+                    if i == j - 1
+                    else lower.astype(jnp.bfloat16)
+                    if i == j + 1
+                    else zero.astype(jnp.bfloat16)
+                )
+                col_band[b, i * LANES : (i + 1) * LANES, j * LANES : (j + 1) * LANES] = block
+            edge = zero
+            if j == half // LANES - 1:
+                edge = jnp.where(side == 0, lower, edge)
+            if j == 0:
+                edge = jnp.where(side == 1, upper, edge)
+            col_band[b, half : half + LANES, j * LANES : (j + 1) * LANES] = edge.astype(
+                jnp.bfloat16
+            )
+
+    terms = coef_ref.shape[3]
+    line = lax.broadcasted_iota(jnp.int32, (3 * rows, terms), 0)
+    term = lax.broadcasted_iota(jnp.int32, (3 * rows, terms), 1)
+    power = line // rows
+    yn = (2.0 * (line % rows).astype(jnp.float32) + 1.0) / rows - 1.0
+    one = jnp.ones_like(yn)
+    none = jnp.zeros_like(yn)
+    constant = jnp.where(term == 0, one, jnp.where(term == 2, yn, jnp.where(term == 5, yn * yn, none)))
+    linear = jnp.where(term == 1, one, jnp.where(term == 4, yn, none))
+    square = jnp.where(term == 3, one, none)
+    vertical = jnp.where(power == 0, constant, jnp.where(power == 1, linear, square))
+    column = lax.broadcasted_iota(jnp.int32, (rows, half), 1) + side * half
+    xn = (2.0 * column.astype(jnp.float32) + 1.0) / (2 * half) - 1.0
+
+    def factors(k, carry):
+        parts = lax.dot_general(
+            vertical,
+            coef_ref[0, k],
+            (((1,), (1,)), ((), ())),
+            precision=lax.Precision.HIGHEST,
+            preferred_element_type=jnp.float32,
+        )
+        start = pl.multiple_of(k * rows, rows)
+        for b in range(basis):
+            p0 = parts[0:rows, b : b + 1]
+            p1 = parts[rows : 2 * rows, b : b + 1]
+            p2 = parts[2 * rows : 3 * rows, b : b + 1]
+            factor[b, pl.ds(start, rows), :] = p0 + xn * (p1 + xn * p2)
+        return carry
+
+    lax.fori_loop(0, count, factors, 0)
+
+    weight_sum = weights_ref[0]
+    for v in range(1, n):
+        weight_sum = weight_sum + weights_ref[v]
+    total = weights_ref[me] * packed[0].astype(jnp.float32)
+    for d in range(1, n):
+        exchange[d - 1].wait_recv()
+        total = total + weights_ref[lax.rem(me - d + n, n)] * received[d].astype(jnp.float32)
+    coadd = (total / jnp.full_like(total, weight_sum)).astype(jnp.bfloat16)
+    templates_ref[0] = coadd
+    library[me] = coadd
+
+    spread = []
+    for d in range(1, n):
+        spread.append(
+            pltpu.make_async_remote_copy(
+                src_ref=library.at[me],
+                dst_ref=library.at[me],
+                send_sem=send2.at[d],
+                recv_sem=recv2.at[d],
+                device_id={"visit": lax.rem(me + d, n)},
+                device_id_type=MESH,
+            )
+        )
+        spread[-1].start()
+
+    near = pl.multiple_of((1 - side) * (half - LANES), LANES)
+    swap = []
+    for d in range(n):
+        source = lax.rem(me - d + n, n)
+        if d:
+            spread[d - 1].wait_recv()
+        swap.append(
+            pltpu.make_async_remote_copy(
+                src_ref=library.at[source, :, pl.ds(near, LANES)],
+                dst_ref=edges.at[source],
+                send_sem=send3.at[d],
+                recv_sem=recv3.at[d],
+                device_id={"tile": 1 - side},
+                device_id_type=MESH,
+            )
+        )
+        swap[-1].start()
+    for k in range(count):
+        chosen[k * rows : (k + 1) * rows, 0:half] = library[slots[k]]
+    for d in range(n):
+        swap[d].wait_recv()
+    for k in range(count):
+        chosen[k * rows : (k + 1) * rows, half : half + LANES] = edges[slots[k]]
+
+    for g in range(groups):
+        tall = jnp.dot(
+            row_band[...],
+            chosen[g * LANES : (g + 1) * LANES, :],
+            preferred_element_type=jnp.float32,
+        ).astype(jnp.bfloat16)
+        for b in range(basis):
+            blurred[b, g * LANES : (g + 1) * LANES, :] = tall[b * LANES : (b + 1) * LANES, :]
+    for g in range(groups):
+        span = slice(g * LANES, (g + 1) * LANES)
+        model = jnp.zeros((LANES, half), jnp.float32)
+        for b in range(basis):
+            smooth = jnp.dot(blurred[b, span, :], col_band[b], preferred_element_type=jnp.float32)
+            model = model + factor[b, span, :] * smooth
+        for k in range(group):
+            model_ref[0, g * group + k] = model[k * rows : (k + 1) * rows, :]
+
+    for copy in exchange + spread + swap:
+        copy.wait_send()
+
+
+def dense_body(science, warped, weights, coef, basis_rows, basis_cols, covered, owner):
+    n = owner.shape[0]
+    unused, count, rows, half = warped.shape
+    basis = basis_rows.shape[0]
+    vmem = pl.BlockSpec(memory_space=pltpu.VMEM)
+    smem = pl.BlockSpec(memory_space=pltpu.SMEM)
+    pixels = count * rows
+    templates, model = pl.pallas_call(
+        functools.partial(match_kernel, n),
+        out_shape=(
+            jax.ShapeDtypeStruct((1, rows, half), jnp.bfloat16),
+            jax.ShapeDtypeStruct((1, count, rows, half), jnp.float32),
+        ),
+        in_specs=[pl.BlockSpec(memory_space=pl.ANY), vmem, vmem, vmem, smem, smem, smem],
+        out_specs=(vmem, vmem),
+        scratch_shapes=[
+            pltpu.VMEM((count, rows, half), jnp.bfloat16),
+            pltpu.VMEM((n, rows, half), jnp.bfloat16),
+            pltpu.VMEM((n, rows, half), jnp.bfloat16),
+            pltpu.VMEM((n, rows, half), jnp.bfloat16),
+            pltpu.VMEM((n, rows, LANES), jnp.bfloat16),
+            pltpu.VMEM((pixels, half + LANES), jnp.bfloat16),
+            pltpu.VMEM((2, 16, LANES), jnp.float32),
+            pltpu.VMEM((basis * LANES, LANES), jnp.bfloat16),
+            pltpu.VMEM((basis, half + LANES, half), jnp.bfloat16),
+            pltpu.VMEM((basis, pixels, half), jnp.float32),
+            pltpu.VMEM((basis, pixels, half + LANES), jnp.bfloat16),
+            pltpu.SemaphoreType.DMA,
+        ]
+        + [pltpu.SemaphoreType.DMA((n,))] * 6,
+        compiler_params=pltpu.CompilerParams(
+            collective_id=0, has_side_effects=True, vmem_limit_bytes=40 * 2**20
+        ),
+    )(warped, coef, basis_rows, basis_cols, weights, covered, owner)
+    return templates, science.astype(jnp.float32) - model
+
+
+def body(science, warped, weights, coef, basis_rows, basis_cols, covered, owner):
+    tiles = owner.shape[0]
+    dense = (
+        covered.shape[1] == tiles
+        and lax.axis_size("visit") == tiles
+        and lax.axis_size("tile") == 2
+    )
+    chosen = dense_body if dense else sparse_body
+    return chosen(science, warped, weights, coef, basis_rows, basis_cols, covered, owner)
+
+
 def solution(mesh):
     in_specs = (
         P(("region", "visit"), None, None, "tile"),

time: 81.8 us -> 23.1 us (0.28)
  blocking collectives: 24.5 us -> 0 us
  Pallas kernels: 0 us -> 19 us
  matrix products: 17.9 us -> 0 us
  starting transfers between devices: 17.9 us -> 0 us
  other arithmetic: 10.7 us -> 0.73 us
  local copies, waits for them, and re-layouts: 6.37 us -> 2.43 us
  waiting for transfers between devices: 2.33 us -> 0 us
    all_gather x1 -> x0, blocking collectives: 24.5 us -> none  [body(): library = lax.all_gather(templates, 'visit', axis=0, tiled=True)]
    pallas_call x0 -> x1, Pallas kernels: none -> 19 us  [dense_body(): pl.pallas_call(functools.partial(match_kernel, n), out_shape=(jax.ShapeDt...]
    dot_general x9 -> x0, matrix products: 17.9 us -> none  [the longest x4 11.5 us: match(): jnp.einsum('kbyx,bxw->kbyw', blurred, col_band, preferred_element_type=jn...]
    ppermute x2 -> x0, starting transfers between devices: 11.4 us -> none  [the longest x1 10.1 us: padded(): lax.ppermute(lax.slice_in_dim(block, 0, width, axis=dim), axis, backward)]
    all_to_all x1 -> x0, starting transfers between devices: 6.49 us -> none  [body(): lax.all_to_all(packed, 'visit', split_axis=0, concat_axis=0, tiled=True)]
    dynamic_update_slice x4 -> x0, other arithmetic: 5.61 us -> none  [body(): lax.map(match, (tpl_blocks, sci_blocks, coef_blocks))]
    all_to_all x1 -> x0, waiting for transfers between devices: 2.1 us -> none  [body(): lax.all_to_all(packed, 'visit', split_axis=0, concat_axis=0, tiled=True)]
    gather x2 -> x0, local copies, waits for them, and re-layouts: 1.85 us -> none  [the longest x1 1.3 us: body(): slot_of = jnp.take(owner, mine_over)]
  transfers between devices with their start and end apart: 3 -> 0, of which waited for: 2 -> 0; matrix products, arithmetic and copies ran while one was open for 6% -> 0% of each run, Pallas kernels for 0% -> 0%
where the time goes in v1:
time: 23.1 us; the launch traced here: 22.9 us
  Pallas kernels  19 us (82%)
  local copies, waits for them, and re-layouts  2.43 us (11%)
  other arithmetic  0.73 us (3%)
  between operations  0.72 us (3%)
    pallas_call x1, Pallas kernels, dense_body(): pl.pallas_call(functools.partial(match_kernel, n), out_shape=(jax.ShapeDt...  19 us
    unnamed x16, local copies, waits for them, and re-layouts  2.43 us
    sub x1, other arithmetic, dense_body(): return (templates, science.astype(jnp.float32) - model)  0.73 us

profile of v1, /device:TPU:1, one launch (start us, length us, event | category | flops | bytes accessed | tf_op | source)
XLA Modules:
  0.0 22.9 jit_solution(12927893265482415127)
XLA Ops:
  0.6 0.0 copy-start.5
  0.6 0.0 copy-start.3
  0.7 0.0 copy-start.2
  0.7 0.0 copy-start.1
  0.7 0.0 copy-start.4
  0.7 0.9 %copy.10.coef_ref = f32[1,8,13,6]{3,2,1,0:T(8,128)S(1)} copy(f32[1,8,13,6]{2,1,3,0:T(8,128)} %param.11) | data formatting | bytes 4992 | tf_op args[3]
  1.6 0.0 copy-done.5
  1.6 0.0 copy-done.3
  1.6 0.0 copy-done.2
  1.6 0.0 copy-done.1
  1.6 0.0 copy-done.4
  1.6 0.0 copy-start
  1.6 0.9 %copy-done = bf16[1,8,32,256]{3,2,1,0:T(8,128)(2,1)S(1)} copy-done((bf16[1,8,32,256]{3,2,1,0:T(8,128)(2,1)S(1)}, bf16[1,8,32,256]{3,2,1,0:T(8,128)(2,1)}, u32[]{:S(2)}) %copy-start) | copy-done | bytes 131096
  2.5 0.0 copy-start.6
  2.5 19.0 %shard_map.95 = (bf16[1,32,256]{2,1,0:T(8,128)(2,1)S(1)}, f32[1,8,32,256]{3,2,1,0:T(8,128)S(1)}) custom-call(bf16[1,8,32,256]{3,2,1,0:T(8,128)(2,1)S(1)} %copy-done, f32[1,8,13,6]{3,2,1,0:T(8,128)S(1)} %copy.10.coef_ref, bf16[13,17]{1,0:T(8,128)(2,1)S(1)} %copy-done.1, bf16[13,17]{1,0:T(8,128)(2,1)S(1)} %copy-done.2, f32[8]{0:T(128)S(1)} %copy-done.4, ...), custom_call_target="tpu_custom_call" | custom-call | tf_op jit(solution)/shard_map/pallas_call | solution.py:322
  21.5 0.0 copy-done.6
  21.5 0.7 %convert_subtract_fusion = f32[1,8,32,256]{3,2,1,0:T(8,128)} fusion(f32[1,8,32,256]{3,2,1,0:T(8,128)S(1)} %get-tuple-element.5, bf16[1,8,32,256]{3,2,1,0:T(8,128)(2,1)S(1)} %copy-done.6), kind=kLoop, calls=%fused_computation | loop fusion | flops 131072 | bytes 655360 | tf_op jit(solution)/shard_map/sub | solution.py:349
  22.3 0.6 %copy.12 = bf16[1,32,256]{2,1,0:T(8,128)(2,1)} copy(bf16[1,32,256]{2,1,0:T(8,128)(2,1)S(1)} %get-tuple-element.8) | data formatting | bytes 32768
Async XLA Ops:
  0.6 1.0 %copy-start.5 = (s32[8]{0:T(128)S(1)}, s32[8]{0:T(128)}, u32[]{:S(2)}) copy-start(s32[8]{0:T(128)} %owner_ref.1) | copy-start | bytes 100
  0.6 0.9 %copy-start.3 = (s32[8,8]{1,0:T(8,128)S(1)}, s32[8,8]{1,0:T(8,128)}, u32[]{:S(2)}) copy-start(s32[8,8]{1,0:T(8,128)} %covered_ref.1) | copy-start | bytes 772
  0.7 0.9 %copy-start.2 = (bf16[13,17]{1,0:T(8,128)(2,1)S(1)}, bf16[13,17]{1,0:T(8,128)(2,1)}, u32[]{:S(2)}) copy-start(bf16[13,17]{1,0:T(8,128)(2,1)} %cols_ref.1) | copy-start | bytes 1330
  0.7 0.9 %copy-start.1 = (bf16[13,17]{1,0:T(8,128)(2,1)S(1)}, bf16[13,17]{1,0:T(8,128)(2,1)}, u32[]{:S(2)}) copy-start(bf16[13,17]{1,0:T(8,128)(2,1)} %rows_ref.1) | copy-start | bytes 1330
  0.7 0.9 %copy-start.4 = (f32[8]{0:T(128)S(1)}, f32[8]{0:T(128)}, u32[]{:S(2)}) copy-start(f32[8]{0:T(128)} %weights_ref.1) | copy-start | bytes 100
  1.6 0.9 %copy-start = (bf16[1,8,32,256]{3,2,1,0:T(8,128)(2,1)S(1)}, bf16[1,8,32,256]{3,2,1,0:T(8,128)(2,1)}, u32[]{:S(2)}) copy-start(bf16[1,8,32,256]{3,2,1,0:T(8,128)(2,1)} %warped_hbm.1) | copy-start | bytes 393220
  2.5 19.0 %copy-start.6 = (bf16[1,8,32,256]{3,2,1,0:T(8,128)(2,1)S(1)}, bf16[1,8,32,256]{3,2,1,0:T(8,128)(2,1)}, u32[]{:S(2)}) copy-start(bf16[1,8,32,256]{3,2,1,0:T(8,128)(2,1)} %param.8) | copy-start | bytes 393220

commit v2 on v1

--- a/solution.py
+++ b/solution.py
@@ -66,7 +66,10 @@
     mine_weight = lax.dynamic_slice_in_dim(slot_weight, visit_here * tile_dev, tile_dev, 0)
     templates = (total / mine_weight[:, None]).astype(jnp.bfloat16).reshape(tile_dev, rows, half)
     library = lax.all_gather(templates, "visit", axis=0, tiled=True)
-    chosen = jnp.take(library, slot_of, axis=0)
+    picks = jnp.dot(
+        select.T, library.reshape(tiles, rows * half), preferred_element_type=jnp.float32
+    )
+    chosen = picks.astype(jnp.bfloat16).reshape(count, rows, half)
     chosen = padded(chosen, (("tile", 2),), reach)
     row_offsets = lax.iota(jnp.int32, rows)[None, :] - lax.iota(jnp.int32, rows)[:, None] + reach
     row_band = band_matrix(basis_rows, row_offsets)
@@ -94,15 +97,21 @@
 def match_kernel(
     n,
     warped_hbm,
+    coef_hbm,
+    rows_hbm,
+    cols_hbm,
+    weights_hbm,
+    covered_hbm,
+    owner_hbm,
+    templates_ref,
+    model_ref,
+    warped,
     coef_ref,
     rows_ref,
     cols_ref,
     weights_ref,
     covered_ref,
     owner_ref,
-    templates_ref,
-    model_ref,
-    warped,
     packed,
     received,
     library,
@@ -129,19 +138,45 @@
     group = LANES // rows
     groups = count // group
 
-    load = pltpu.make_async_copy(warped_hbm.at[0], warped, load_sem)
-    load.start()
+    def partner(d):
+        x, z = me % 2, me // 2
+        across = d % 2
+        over = [d // 2 // 2**bit % 2 for bit in range(8)]
+        there = 0
+        for bit in range(8):
+            digit = z // 2**bit % 2
+            there = there + 2**bit * (1 - digit if over[bit] else digit)
+        return 2 * there + (1 - x if across else x)
+
+    order = list(range(n - 1, 0, -1))
     barrier = pltpu.get_barrier_semaphore()
-    for d in range(1, n):
+    for d in order:
         pl.semaphore_signal(
-            barrier, inc=1, device_id={"visit": lax.rem(me + d, n)}, device_id_type=MESH
+            barrier, inc=1, device_id={"visit": partner(d)}, device_id_type=MESH
         )
     pl.semaphore_signal(barrier, inc=1, device_id={"tile": 1 - side}, device_id_type=MESH)
 
+    loads = [
+        pltpu.make_async_copy(source, target, load_sem.at[i])
+        for i, (source, target) in enumerate(
+            (
+                (covered_hbm, covered_ref),
+                (owner_hbm, owner_ref),
+                (warped_hbm.at[0], warped),
+                (weights_hbm, weights_ref),
+                (rows_hbm, rows_ref),
+                (cols_hbm, cols_ref),
+                (coef_hbm, coef_ref),
+            )
+        )
+    ]
+    for load in loads:
+        load.start()
+    for load in loads[:3]:
+        load.wait()
     slots = [owner_ref[covered_ref[me, k]] for k in range(count)]
-    load.wait()
     for d in range(n):
-        target = lax.rem(me + d, n)
+        target = partner(d)
         k_of = jnp.int32(0)
         for k in range(1, count):
             k_of = jnp.where(slots[k] == target, jnp.int32(k), k_of)
@@ -149,19 +184,21 @@
     pl.semaphore_wait(barrier, n)
 
     exchange = []
-    for d in range(1, n):
+    for d in order:
         exchange.append(
             pltpu.make_async_remote_copy(
                 src_ref=packed.at[d],
                 dst_ref=received.at[d],
                 send_sem=send1.at[d],
                 recv_sem=recv1.at[d],
-                device_id={"visit": lax.rem(me + d, n)},
+                device_id={"visit": partner(d)},
                 device_id_type=MESH,
             )
         )
         exchange[-1].start()
 
+    for load in loads[3:]:
+        load.wait()
     profiles[...] = jnp.zeros_like(profiles)
     profiles[0, 0:basis, 0:ksize] = rows_ref[...].astype(jnp.float32)
     profiles[1, 0:basis, 0:ksize] = cols_ref[...].astype(jnp.float32)
@@ -210,33 +247,19 @@
                 jnp.bfloat16
             )
 
-    terms = coef_ref.shape[3]
-    line = lax.broadcasted_iota(jnp.int32, (3 * rows, terms), 0)
-    term = lax.broadcasted_iota(jnp.int32, (3 * rows, terms), 1)
-    power = line // rows
-    yn = (2.0 * (line % rows).astype(jnp.float32) + 1.0) / rows - 1.0
-    one = jnp.ones_like(yn)
-    none = jnp.zeros_like(yn)
-    constant = jnp.where(term == 0, one, jnp.where(term == 2, yn, jnp.where(term == 5, yn * yn, none)))
-    linear = jnp.where(term == 1, one, jnp.where(term == 4, yn, none))
-    square = jnp.where(term == 3, one, none)
-    vertical = jnp.where(power == 0, constant, jnp.where(power == 1, linear, square))
+    line = lax.broadcasted_iota(jnp.int32, (rows, 1), 0)
+    yn = (2.0 * line.astype(jnp.float32) + 1.0) / rows - 1.0
     column = lax.broadcasted_iota(jnp.int32, (rows, half), 1) + side * half
     xn = (2.0 * column.astype(jnp.float32) + 1.0) / (2 * half) - 1.0
 
     def factors(k, carry):
-        parts = lax.dot_general(
-            vertical,
-            coef_ref[0, k],
-            (((1,), (1,)), ((), ())),
-            precision=lax.Precision.HIGHEST,
-            preferred_element_type=jnp.float32,
-        )
+        c = [coef_ref[0, p, pl.ds(k, 1), :] for p in range(coef_ref.shape[1])]
+        constant = c[0] + yn * (c[2] + yn * c[5])
+        linear = c[1] + yn * c[4]
+        square = c[3]
         start = pl.multiple_of(k * rows, rows)
         for b in range(basis):
-            p0 = parts[0:rows, b : b + 1]
-            p1 = parts[rows : 2 * rows, b : b + 1]
-            p2 = parts[2 * rows : 3 * rows, b : b + 1]
+            p0, p1, p2 = (p[:, b : b + 1] for p in (constant, linear, square))
             factor[b, pl.ds(start, rows), :] = p0 + xn * (p1 + xn * p2)
         return carry
 
@@ -247,32 +270,32 @@
         weight_sum = weight_sum + weights_ref[v]
     total = weights_ref[me] * packed[0].astype(jnp.float32)
     for d in range(1, n):
-        exchange[d - 1].wait_recv()
-        total = total + weights_ref[lax.rem(me - d + n, n)] * received[d].astype(jnp.float32)
+        exchange[order.index(d)].wait_recv()
+        total = total + weights_ref[partner(d)] * received[d].astype(jnp.float32)
     coadd = (total / jnp.full_like(total, weight_sum)).astype(jnp.bfloat16)
-    templates_ref[0] = coadd
     library[me] = coadd
 
     spread = []
-    for d in range(1, n):
+    for d in order:
         spread.append(
             pltpu.make_async_remote_copy(
                 src_ref=library.at[me],
                 dst_ref=library.at[me],
                 send_sem=send2.at[d],
                 recv_sem=recv2.at[d],
-                device_id={"visit": lax.rem(me + d, n)},
+                device_id={"visit": partner(d)},
                 device_id_type=MESH,
             )
         )
         spread[-1].start()
 
+    templates_ref[0] = coadd
     near = pl.multiple_of((1 - side) * (half - LANES), LANES)
     swap = []
     for d in range(n):
-        source = lax.rem(me - d + n, n)
+        source = partner(d)
         if d:
-            spread[d - 1].wait_recv()
+            spread[order.index(d)].wait_recv()
         swap.append(
             pltpu.make_async_remote_copy(
                 src_ref=library.at[source, :, pl.ds(near, LANES)],
@@ -317,7 +340,6 @@
     unused, count, rows, half = warped.shape
     basis = basis_rows.shape[0]
     vmem = pl.BlockSpec(memory_space=pltpu.VMEM)
-    smem = pl.BlockSpec(memory_space=pltpu.SMEM)
     pixels = count * rows
     templates, model = pl.pallas_call(
         functools.partial(match_kernel, n),
@@ -325,10 +347,16 @@
             jax.ShapeDtypeStruct((1, rows, half), jnp.bfloat16),
             jax.ShapeDtypeStruct((1, count, rows, half), jnp.float32),
         ),
-        in_specs=[pl.BlockSpec(memory_space=pl.ANY), vmem, vmem, vmem, smem, smem, smem],
+        in_specs=[pl.BlockSpec(memory_space=pl.ANY)] * 7,
         out_specs=(vmem, vmem),
         scratch_shapes=[
             pltpu.VMEM((count, rows, half), jnp.bfloat16),
+            pltpu.VMEM((1, coef.shape[3], count, basis), jnp.float32),
+            pltpu.VMEM(basis_rows.shape, jnp.bfloat16),
+            pltpu.VMEM(basis_cols.shape, jnp.bfloat16),
+            pltpu.SMEM(weights.shape, jnp.float32),
+            pltpu.SMEM(covered.shape, jnp.int32),
+            pltpu.SMEM(owner.shape, jnp.int32),
             pltpu.VMEM((n, rows, half), jnp.bfloat16),
             pltpu.VMEM((n, rows, half), jnp.bfloat16),
             pltpu.VMEM((n, rows, half), jnp.bfloat16),
@@ -339,13 +367,26 @@
             pltpu.VMEM((basis, half + LANES, half), jnp.bfloat16),
             pltpu.VMEM((basis, pixels, half), jnp.float32),
             pltpu.VMEM((basis, pixels, half + LANES), jnp.bfloat16),
-            pltpu.SemaphoreType.DMA,
+            pltpu.SemaphoreType.DMA((7,)),
         ]
         + [pltpu.SemaphoreType.DMA((n,))] * 6,
         compiler_params=pltpu.CompilerParams(
             collective_id=0, has_side_effects=True, vmem_limit_bytes=40 * 2**20
         ),
-    )(warped, coef, basis_rows, basis_cols, weights, covered, owner)
+    )(
+        *(
+            pltpu.with_memory_space_constraint(operand, pltpu.HBM)
+            for operand in (
+                warped,
+                jnp.transpose(coef, (0, 3, 1, 2)),
+                basis_rows,
+                basis_cols,
+                weights,
+                covered,
+                owner,
+            )
+        )
+    )
     return templates, science.astype(jnp.float32) - model
 
 

time: 23.1 us -> 20 us (0.87)
  local copies, waits for them, and re-layouts: 2.43 us -> 0.61 us
  Pallas kernels: 19 us -> 17.8 us
    unnamed x16 -> x3, local copies, waits for them, and re-layouts: 2.43 us -> 0.61 us
    pallas_call x1, Pallas kernels: 19 us -> 17.8 us  [dense_body(): pl.pallas_call(functools.partial(match_kernel, n), out_shape=(jax.ShapeDt...]
where the time goes in v2:
time: 20 us; the launch traced here: 19.8 us
  Pallas kernels  17.8 us (89%)
  other arithmetic  0.73 us (4%)
  between operations  0.66 us (3%)
  local copies, waits for them, and re-layouts  0.61 us (3%)
    pallas_call x1, Pallas kernels, dense_body(): pl.pallas_call(functools.partial(match_kernel, n), out_shape=(jax.ShapeDt...  17.8 us
    sub x1, other arithmetic, dense_body(): return (templates, science.astype(jnp.float32) - model)  0.73 us
    unnamed x3, local copies, waits for them, and re-layouts  0.61 us

profile of v2, /device:TPU:1, one launch (start us, length us, event | category | flops | bytes accessed | tf_op | source)
XLA Modules:
  0.0 19.8 jit_solution(14520434578987707223)
XLA Ops:
  0.6 0.0 copy-start
  0.6 17.8 %shard_map.95 = (bf16[1,32,256]{2,1,0:T(8,128)(2,1)S(1)}, f32[1,8,32,256]{3,2,1,0:T(8,128)S(1)}) custom-call(bf16[1,8,32,256]{3,2,1,0:T(8,128)(2,1)} %warped_hbm.1, f32[1,6,8,13]{3,2,1,0:T(8,128)} %bitcast.1, bf16[13,17]{1,0:T(8,128)(2,1)} %rows_hbm.1, bf16[13,17]{1,0:T(8,128)(2,1)} %cols_hbm.1, f32[8]{0:T(128)} %weights_hbm.1, s32[8,8]{1,0:T(8,128)} %covered_hbm.1, ...), custom_call_target="tpu_custom_call" | custom-call | tf_op jit(solution)/shard_map/pallas_call | solution.py:344
  18.5 0.0 copy-done
  18.5 0.7 %convert_subtract_fusion = f32[1,8,32,256]{3,2,1,0:T(8,128)} fusion(f32[1,8,32,256]{3,2,1,0:T(8,128)S(1)} %get-tuple-element.5, bf16[1,8,32,256]{3,2,1,0:T(8,128)(2,1)S(1)} %copy-done), kind=kLoop, calls=%fused_computation | loop fusion | flops 131072 | bytes 655360 | tf_op jit(solution)/shard_map/sub | solution.py:390
  19.2 0.6 %copy.11 = bf16[1,32,256]{2,1,0:T(8,128)(2,1)} copy(bf16[1,32,256]{2,1,0:T(8,128)(2,1)S(1)} %get-tuple-element.8) | data formatting | bytes 32768
Async XLA Ops:
  0.6 17.8 %copy-start = (bf16[1,8,32,256]{3,2,1,0:T(8,128)(2,1)S(1)}, bf16[1,8,32,256]{3,2,1,0:T(8,128)(2,1)}, u32[]{:S(2)}) copy-start(bf16[1,8,32,256]{3,2,1,0:T(8,128)(2,1)} %param.8) | copy-start | bytes 393220

commit v3 on v2

--- a/solution.py
+++ b/solution.py
@@ -309,19 +309,25 @@
         swap[-1].start()
     for k in range(count):
         chosen[k * rows : (k + 1) * rows, 0:half] = library[slots[k]]
+
+    def blur(columns):
+        for g in range(groups):
+            tall = jnp.dot(
+                row_band[...],
+                chosen[g * LANES : (g + 1) * LANES, columns],
+                preferred_element_type=jnp.float32,
+            ).astype(jnp.bfloat16)
+            for b in range(basis):
+                blurred[b, g * LANES : (g + 1) * LANES, columns] = tall[
+                    b * LANES : (b + 1) * LANES, :
+                ]
+
+    blur(slice(0, half))
     for d in range(n):
         swap[d].wait_recv()
     for k in range(count):
         chosen[k * rows : (k + 1) * rows, half : half + LANES] = edges[slots[k]]
-
-    for g in range(groups):
-        tall = jnp.dot(
-            row_band[...],
-            chosen[g * LANES : (g + 1) * LANES, :],
-            preferred_element_type=jnp.float32,
-        ).astype(jnp.bfloat16)
-        for b in range(basis):
-            blurred[b, g * LANES : (g + 1) * LANES, :] = tall[b * LANES : (b + 1) * LANES, :]
+    blur(slice(half, half + LANES))
     for g in range(groups):
         span = slice(g * LANES, (g + 1) * LANES)
         model = jnp.zeros((LANES, half), jnp.float32)

time: 20 us -> 19.5 us (0.975)
  Pallas kernels: 17.8 us -> 17.4 us
    pallas_call x1, Pallas kernels: 17.8 us -> 17.4 us  [dense_body(): pl.pallas_call(functools.partial(match_kernel, n), out_shape=(jax.ShapeDt...]
where the time goes in v3:
time: 19.5 us; the launch traced here: 19.4 us
  Pallas kernels  17.4 us (89%)
  other arithmetic  0.73 us (4%)
  between operations  0.66 us (3%)
  local copies, waits for them, and re-layouts  0.61 us (3%)
    pallas_call x1, Pallas kernels, dense_body(): pl.pallas_call(functools.partial(match_kernel, n), out_shape=(jax.ShapeDt...  17.4 us
    sub x1, other arithmetic, dense_body(): return (templates, science.astype(jnp.float32) - model)  0.73 us
    unnamed x3, local copies, waits for them, and re-layouts  0.61 us

profile of v3, /device:TPU:1, one launch (start us, length us, event | category | flops | bytes accessed | tf_op | source)
XLA Modules:
  0.0 19.4 jit_solution(18141932307309247082)
XLA Ops:
  0.6 0.0 copy-start
  0.6 17.4 %shard_map.95 = (bf16[1,32,256]{2,1,0:T(8,128)(2,1)S(1)}, f32[1,8,32,256]{3,2,1,0:T(8,128)S(1)}) custom-call(bf16[1,8,32,256]{3,2,1,0:T(8,128)(2,1)} %warped_hbm.1, f32[1,6,8,13]{3,2,1,0:T(8,128)} %bitcast.1, bf16[13,17]{1,0:T(8,128)(2,1)} %rows_hbm.1, bf16[13,17]{1,0:T(8,128)(2,1)} %cols_hbm.1, f32[8]{0:T(128)} %weights_hbm.1, s32[8,8]{1,0:T(8,128)} %covered_hbm.1, ...), custom_call_target="tpu_custom_call" | custom-call | tf_op jit(solution)/shard_map/pallas_call | solution.py:350
  18.0 0.0 copy-done
  18.0 0.7 %convert_subtract_fusion = f32[1,8,32,256]{3,2,1,0:T(8,128)} fusion(f32[1,8,32,256]{3,2,1,0:T(8,128)S(1)} %get-tuple-element.5, bf16[1,8,32,256]{3,2,1,0:T(8,128)(2,1)S(1)} %copy-done), kind=kLoop, calls=%fused_computation | loop fusion | flops 131072 | bytes 655360 | tf_op jit(solution)/shard_map/sub | solution.py:396
  18.8 0.6 %copy.11 = bf16[1,32,256]{2,1,0:T(8,128)(2,1)} copy(bf16[1,32,256]{2,1,0:T(8,128)(2,1)S(1)} %get-tuple-element.8) | data formatting | bytes 32768
Async XLA Ops:
  0.6 17.4 %copy-start = (bf16[1,8,32,256]{3,2,1,0:T(8,128)(2,1)S(1)}, bf16[1,8,32,256]{3,2,1,0:T(8,128)(2,1)}, u32[]{:S(2)}) copy-start(bf16[1,8,32,256]{3,2,1,0:T(8,128)(2,1)} %param.8) | copy-start | bytes 393220
